TPU v7x, 32 devices: a whole 2x2x4 slice. The times are simulated.
32 devices in a mesh: lon: 4 (over z), grp: 8 (over y, x, core).
Axes of the slice: x: 2, y: 2, z: 4, core: 2. Of those that a mesh axis runs over, the one named last changes fastest.
Arguments:
- columns: bfloat16 [32768, 512], P(('lon', 'grp')), may hold values from -6 to 6
- cos_zenith: bfloat16 [32768], P(('lon', 'grp')), may hold values from 0.049804688 to 1
- sunlit: int32 [32768], P(('lon', 'grp')), may hold values from 0 to 1, as said below
- span_map: int32 [32768], P(('lon', 'grp')), may hold values from 0 to 1023, as said below
- w_in: bfloat16 [512, 1024], replicated, may hold values from -0.25 to 0.25
- w_mid: bfloat16 [1024, 1024], replicated, may hold values from -0.1875 to 0.1875
- w_out: bfloat16 [1024, 256], replicated, may hold values from -0.1875 to 0.1875
Outputs:
- sw_heating: bfloat16 [32768, 128], P(('lon', 'grp'))
- sw_flux: float32 [32768, 128], P(('lon', 'grp'))
Inputs may be any that keep to these rules, and one draw needn't show every extreme that they name: Within each block, span_map is a permutation of 0 to 1023. All 128-slot pieces of span_map in all blocks of one strip hold the same number of sunlit columns; that number for strip l and for strip (l + 2) mod 4 add up to 128; in some strip every column is sunlit.
All inputs are finite; a program needn't handle non-finite values.
Results may differ from a plain program's by a relative error of at most 0.0059.
Values may be sent and summed in bfloat16 or wider, within the bound.
A program may use at most 64 MiB of HBM per device.

v0:
```python
import jax
import jax.numpy as jnp
from jax import lax
from jax.sharding import PartitionSpec as P


def network(row_block, w_in, w_mid, w_out):
    layer_one = jax.nn.silu(jnp.dot(row_block, w_in, preferred_element_type=jnp.float32)).astype(
        jnp.bfloat16
    )
    layer_two = jax.nn.silu(jnp.dot(layer_one, w_mid, preferred_element_type=jnp.float32)).astype(
        jnp.bfloat16
    )
    return jnp.dot(layer_two, w_out, preferred_element_type=jnp.float32)


def run_network(phys_rows, w_in, w_mid, w_out):
    return network(phys_rows, w_in, w_mid, w_out)


def body(columns, cos_zenith, sunlit, span_map, w_in, w_mid, w_out):
    row_count = columns.shape[0]
    groups = lax.axis_size("grp")
    piece_len = row_count // groups
    levels = w_out.shape[1] // 2
    arrived = (
        lax.all_to_all(
            columns[span_map].reshape(groups, piece_len, columns.shape[1]),
            "grp",
            split_axis=0,
            concat_axis=0,
            tiled=True,
        ),
        lax.all_to_all(
            cos_zenith[span_map].reshape(groups, piece_len),
            "grp",
            split_axis=0,
            concat_axis=0,
            tiled=True,
        ),
        lax.all_to_all(
            sunlit[span_map].reshape(groups, piece_len),
            "grp",
            split_axis=0,
            concat_axis=0,
            tiled=True,
        ),
    )
    phys_rows = arrived[0].reshape(row_count, columns.shape[1])
    cos_phys = arrived[1].reshape(row_count)
    sun_phys = arrived[2].reshape(row_count)
    outputs = run_network(phys_rows, w_in, w_mid, w_out)
    insolation = sun_phys.astype(jnp.float32) * cos_phys.astype(jnp.float32)
    phys_heating = (insolation[:, None] * outputs[:, :levels]).astype(jnp.bfloat16)
    flux_out = insolation[:, None] * jax.nn.softplus(outputs[:, levels:])
    returned = lax.all_to_all(
        phys_heating.reshape(groups, piece_len, levels),
        "grp",
        split_axis=0,
        concat_axis=0,
        tiled=True,
    )
    returned = returned.reshape(row_count, levels)
    heating = jnp.zeros_like(returned).at[span_map].set(returned)
    return (heating, flux_out)


def solution(mesh):
    in_specs = (
        P(("lon", "grp"), None),
        P(("lon", "grp")),
        P(("lon", "grp")),
        P(("lon", "grp")),
        P(),
        P(),
        P(),
    )
    out_specs = (P(("lon", "grp"), None), P(("lon", "grp"), None))
    return jax.shard_map(body, mesh=mesh, in_specs=in_specs, out_specs=out_specs, check_vma=False)
```

profile of v0, /device:TPU:0, one launch (start us, length us, event | category | flops | bytes accessed | tf_op | source)
XLA Modules:
  0.0 76.0 jit_solution(15321397326410753050)
XLA Ops:
  0.6 0.0 copy-start
  0.6 0.0 copy-start.1
  0.7 0.0 copy-start.2
  0.7 0.8 %broadcast_clamp_fusion = (s32[1024]{0:T(1024)S(1)}, s32[1024]{0:T(1024)S(1)}) fusion(s32[1024]{0:T(1024)} %param.10), kind=kLoop, calls=%fused_computation.17 | loop fusion | flops 4096 | bytes 12288 | tf_op jit(solution)/shard_map/gather | solution.py:42
  1.5 6.4 %gather_fusion.1 = bf16[1024]{0:T(1024)(128)(2,1)S(1)} fusion(bf16[1024]{0:T(1024)(128)(2,1)} %param.8, s32[1024]{0:T(1024)S(1)} %get-tuple-element.4), kind=kCustom, calls=%fused_computation.1 | custom fusion | bytes 8192 | tf_op jit(solution)/shard_map/gather | solution.py:35
  7.9 0.6 copy.9
  8.5 5.2 %all-to-all-start.1 = ((bf16[8,1,128]{2,1,0:T(2,128)(2,1)}), bf16[8,1,128]{2,1,0:T(2,128)(2,1)S(1)}, u32[]{:S(2)}, u32[]{:S(2)}) async-start(bf16[8,1,128]{2,1,0:T(2,128)(2,1)} %copy.9), calls=%async_computation.1 | async-start | bytes 8192 | tf_op jit(solution)/shard_map/all_to_all | solution.py:34
  13.7 0.0 copy-done.1
  13.7 8.8 %gather_fusion = s32[1024]{0:T(1024)} fusion(s32[1024]{0:T(1024)S(1)} %copy-done.1, s32[1024]{0:T(1024)S(1)} %get-tuple-element.4), kind=kCustom, calls=%fused_computation | custom fusion | bytes 12288 | tf_op jit(solution)/shard_map/gather | solution.py:42
  22.5 0.0 all-to-all-done.1
  22.5 4.2 %all-to-all-start = ((s32[8,1,128]{2,1,0:T(1,128)}), s32[8,1,128]{2,1,0:T(1,128)S(1)}, u32[]{:S(2)}, u32[]{:S(2)}) async-start(s32[8,1,128]{2,1,0:T(1,128)} %bitcast), calls=%async_computation | async-start | bytes 8192 | tf_op jit(solution)/shard_map/all_to_all | solution.py:41
  26.7 0.0 copy-done.2
  26.7 5.1 %gather_fusion.2 = bf16[1024,512]{1,0:T(8,128)(2,1)} fusion(bf16[1024,512]{1,0:T(8,128)(2,1)S(1)} %copy-done.2, s32[1024]{0:T(1024)S(1)} %get-tuple-element.4), kind=kCustom, calls=%fused_computation.2 | custom fusion | bytes 2101248 | tf_op jit(solution)/shard_map/gather | solution.py:28
  31.8 0.0 all-to-all-done
  31.8 4.2 %all-to-all-start.2 = ((bf16[8,128,512]{2,1,0:T(8,128)(2,1)}), bf16[8,128,512]{2,1,0:T(8,128)(2,1)S(1)}, u32[]{:S(2)}, u32[]{:S(2)}) async-start(bf16[8,128,512]{2,1,0:T(8,128)(2,1)} %bitcast.12), calls=%async_computation.2 | async-start | bytes 2097152 | tf_op jit(solution)/shard_map/all_to_all | solution.py:27
  36.0 15.4 %all-to-all-done.2 = bf16[8,128,512]{2,1,0:T(8,128)(2,1)S(1)} async-done(((bf16[8,128,512]{2,1,0:T(8,128)(2,1)}), bf16[8,128,512]{2,1,0:T(8,128)(2,1)S(1)}, u32[]{:S(2)}, u32[]{:S(2)}) %all-to-all-start.2) | async-done | bytes 1048608 | tf_op jit(solution)/shard_map/all_to_all | solution.py:27
  51.4 0.0 copy-done
  51.4 6.8 %fusion = f32[1024,1024]{1,0:T(8,128)} fusion(bf16[1024,1024]{1,0:T(8,128)(2,1)S(1)} %copy-done, bf16[1024,512]{1,0:T(8,128)(2,1)S(1)} %bitcast.14, bf16[512,1024]{1,0:T(8,128)(2,1)} %param.11), kind=kOutput, calls=%fused_computation.6 | convolution fusion | flops 3226468352 | bytes 8388608 | tf_op jit(solution)/shard_map/dot_general | solution.py:11
  58.2 3.5 %fusion.1 = f32[1024,256]{1,0:T(8,128)S(1)} fusion(bf16[1024,256]{1,0:T(8,128)(2,1)} %param.13, f32[1024,1024]{1,0:T(8,128)} %fusion), kind=kOutput, calls=%fused_computation.7 | convolution fusion | flops 542113792 | bytes 5767168 | tf_op jit(solution)/shard_map/dot_general | solution.py:14
  61.7 1.1 %fusion.4 = (f32[1024,128]{1,0:T(8,128)}, bf16[1024,128]{1,0:T(8,128)(2,1)S(1)}) fusion(f32[1024,256]{1,0:T(8,128)S(1)} %fusion.1, f32[1024]{0:T(1024)S(1)} %bitcast.16), kind=kLoop, calls=%fused_computation.10 | loop fusion | flops 1179648 | bytes 1839104 | tf_op jit(solution)/shard_map/mul | solution.py:55
  62.9 9.3 %all_to_all.28 = bf16[8,128,128]{2,1,0:T(8,128)(2,1)S(1)} all-to-all(bf16[8,128,128]{2,1,0:T(8,128)(2,1)S(1)} %bitcast.13), channel_id=1, replica_groups=mesh['lon'=4,'grp'=8] {'grp'}, dimensions={0} | all-to-all | bytes 524288 | tf_op jit(solution)/shard_map/all_to_all | solution.py:56
  72.2 3.8 %scatter_custom_fusion = bf16[1024,128]{1,0:T(8,128)(2,1)} fusion(s32[1024]{0:T(1024)S(1)} %get-tuple-element.5, bf16[1024,128]{1,0:T(8,128)(2,1)S(1)} %bitcast.15, bf16[]{:T(256)} %constant.5.clone.1), kind=kCustom, calls=%fused_computation.13 | custom fusion | bytes 262146 | tf_op jit(solution)/shard_map/scatter | solution.py:64
  (1 shorter events, 0.0 us)
Async XLA Ops:
  0.6 50.7 %copy-start = (bf16[1024,1024]{1,0:T(8,128)(2,1)S(1)}, bf16[1024,1024]{1,0:T(8,128)(2,1)}, u32[]{:S(2)}) copy-start(bf16[1024,1024]{1,0:T(8,128)(2,1)} %param.12) | copy-start | bytes 6291460
  0.6 13.0 %copy-start.1 = (s32[1024]{0:T(1024)S(1)}, s32[1024]{0:T(1024)}, u32[]{:S(2)}) copy-start(s32[1024]{0:T(1024)} %param.9) | copy-start | bytes 12292
  0.7 26.1 %copy-start.2 = (bf16[1024,512]{1,0:T(8,128)(2,1)S(1)}, bf16[1024,512]{1,0:T(8,128)(2,1)}, u32[]{:S(2)}) copy-start(bf16[1024,512]{1,0:T(8,128)(2,1)} %param.7) | copy-start | bytes 3145732
  8.5 14.0 %all-to-all-start.1 = ((bf16[8,1,128]{2,1,0:T(2,128)(2,1)}), bf16[8,1,128]{2,1,0:T(2,128)(2,1)S(1)}, u32[]{:S(2)}, u32[]{:S(2)}) async-start(bf16[8,1,128]{2,1,0:T(2,128)(2,1)} %copy.9), calls=%async_computation.1 | async-start | bytes 8192 | tf_op jit(solution)/shard_map/all_to_all | solution.py:34
  22.5 9.3 %all-to-all-start = ((s32[8,1,128]{2,1,0:T(1,128)}), s32[8,1,128]{2,1,0:T(1,128)S(1)}, u32[]{:S(2)}, u32[]{:S(2)}) async-start(s32[8,1,128]{2,1,0:T(1,128)} %bitcast), calls=%async_computation | async-start | bytes 8192 | tf_op jit(solution)/shard_map/all_to_all | solution.py:41
  31.8 19.6 %all-to-all-start.2 = ((bf16[8,128,512]{2,1,0:T(8,128)(2,1)}), bf16[8,128,512]{2,1,0:T(8,128)(2,1)S(1)}, u32[]{:S(2)}, u32[]{:S(2)}) async-start(bf16[8,128,512]{2,1,0:T(8,128)(2,1)} %bitcast.12), calls=%async_computation.2 | async-start | bytes 2097152 | tf_op jit(solution)/shard_map/all_to_all | solution.py:27
where the time goes:
time: 76.4 us; the launch traced here: 76 us
  local copies, waits for them, and re-layouts  24.7 us (32%)
  waiting for transfers between devices  15.4 us (20%)
  starting transfers between devices  13.6 us (18%)
  matrix products  10.4 us (14%)
  blocking collectives  9.33 us (12%)
  other arithmetic  1.98 us (3%)
    all_to_all x1, waiting for transfers between devices, body(): lax.all_to_all(columns[span_map].reshape(groups, piece_len, columns.shape...  15.4 us
    all_to_all x1, blocking collectives, body(): lax.all_to_all(phys_heating.reshape(groups, piece_len, levels), 'grp', sp...  9.33 us
    gather x1, local copies, waits for them, and re-layouts, body(): sunlit[span_map].reshape(groups, piece_len)  8.84 us
    dot_general x1, matrix products, network(): jnp.dot(layer_one, w_mid, preferred_element_type=jnp.float32)  6.83 us
    gather x1, local copies, waits for them, and re-layouts, body(): cos_zenith[span_map].reshape(groups, piece_len)  6.38 us
    all_to_all x1, starting transfers between devices, body(): lax.all_to_all(cos_zenith[span_map].reshape(groups, piece_len), 'grp', sp...  5.17 us
    gather x1, local copies, waits for them, and re-layouts, body(): columns[span_map].reshape(groups, piece_len, columns.shape[1])  5.05 us
    all_to_all x1, starting transfers between devices, body(): lax.all_to_all(columns[span_map].reshape(groups, piece_len, columns.shape...  4.19 us
  transfers between devices with their start and end apart: 3, of which 1 were waited for; matrix products, arithmetic and copies ran while one was open for 18% of the time, Pallas kernels for 0%

commit v1 on v0

v1 whole, which is shorter than its diff:
```python
import functools

import jax
import jax.numpy as jnp
from jax import lax
from jax.experimental import pallas as pl
from jax.experimental.pallas import tpu as pltpu
from jax.sharding import PartitionSpec as P

MESH = pl.DeviceIdType.MESH
LANES = 128
ROWS = 256
WIDE = 256
PARTS = 4


def silu(v):
    half = 0.5 * v
    return half + half * jnp.tanh(half)


def softplus(v):
    return jnp.maximum(v, 0.0) + jnp.log(1.0 + jnp.exp(-jnp.abs(v)))


def down(row):
    return jnp.transpose(jnp.broadcast_to(row, (LANES, LANES)))


def kernel(
    groups,
    columns_hbm, cos_hbm, sun_hbm, map_hbm, w_in_hbm, w_mid_hbm, w_out_hbm,
    heat_hbm, flux_hbm,
    columns, cos, sun, smap, w_in, w_mid, w_out,
    onehot, insol, layer_one, layer_two, heat, flux, leaving,
    load_sem, heat_sem, own_sem, send_sem, recv_sem,
):
    rows = columns.shape[0]
    hidden = w_in.shape[1]
    levels = heat.shape[1]
    piece = rows // groups
    per = groups // PARTS
    part_rows = rows // PARTS
    me = lax.axis_index("grp")
    my_part, my_place = me // per, lax.rem(me, per)

    barrier = pltpu.get_barrier_semaphore()
    for off in range(1, groups):
        pl.semaphore_signal(
            barrier, inc=1, device_id={"grp": lax.rem(me + off, groups)}, device_id_type=MESH
        )

    pairs = (
        (map_hbm, smap), (cos_hbm, cos), (sun_hbm, sun),
        (w_in_hbm, w_in), (columns_hbm, columns), (w_mid_hbm, w_mid), (w_out_hbm, w_out),
    )
    loads = [
        pltpu.make_async_copy(src, dst, load_sem.at[at]) for at, (src, dst) in enumerate(pairs)
    ]
    for load in loads:
        load.start()

    for load in loads[:3]:
        load.wait()
    slots = smap[...].astype(jnp.float32)
    light = sun[...].astype(jnp.float32) * cos[...].astype(jnp.float32)
    lane = lax.broadcasted_iota(jnp.int32, (LANES, LANES), 1).astype(jnp.float32)
    for at in range(rows // LANES):
        here = pl.ds(at * LANES, LANES)
        insol[here, :] = down(light[at : at + 1, :])
        wanted = down(slots[at : at + 1, :])
        for k in range(rows // LANES):
            onehot[here, k * LANES : (k + 1) * LANES] = jnp.where(
                wanted == lane + float(k * LANES), 1.0, 0.0
            ).astype(jnp.bfloat16)

    loads[3].wait()
    loads[4].wait()
    heat_copies = []
    for at in range(rows // ROWS):
        here = pl.ds(at * ROWS, ROWS)
        for n in range(0, hidden, WIDE):
            layer_one[at % 2, :, n : n + WIDE] = silu(
                jnp.dot(columns[here, :], w_in[:, n : n + WIDE], preferred_element_type=jnp.float32)
            ).astype(jnp.bfloat16)
        if at == 0:
            loads[5].wait()
        for n in range(0, hidden, WIDE):
            layer_two[at % 2, :, n : n + WIDE] = silu(
                jnp.dot(layer_one[at % 2], w_mid[:, n : n + WIDE], preferred_element_type=jnp.float32)
            ).astype(jnp.bfloat16)
        if at == 0:
            loads[6].wait()
        out = jnp.dot(layer_two[at % 2], w_out[...], preferred_element_type=jnp.float32)
        heat[here, :] = (insol[here, :] * out[:, :levels]).astype(jnp.bfloat16)
        flux[here, :] = (insol[here, :] * softplus(out[:, levels:])).astype(jnp.bfloat16)
        copy = pltpu.make_async_copy(heat.at[here, :], heat_hbm.at[here, :], heat_sem.at[at])
        copy.start()
        heat_copies.append(copy)

    pl.semaphore_wait(barrier, groups - 1)
    copies = []
    own = None
    arriving = pl.ds(pl.multiple_of(me * piece, piece), piece)
    for k in range(PARTS):
        part = lax.rem(my_part + k + 1, PARTS)
        here = pl.ds(pl.multiple_of(part * part_rows, part_rows), part_rows)
        leaving[here, :] = jnp.dot(
            onehot[here, :], flux[...], preferred_element_type=jnp.float32
        ).astype(jnp.bfloat16)
        for j in range(per):
            to = part * per + lax.rem(my_place + j, per)
            source = leaving.at[pl.ds(pl.multiple_of(to * piece, piece), piece), :]
            if k == PARTS - 1 and j == 0:
                own = pltpu.make_async_copy(source, flux_hbm.at[arriving, :], own_sem)
                own.start()
                continue
            copy = pltpu.make_async_remote_copy(
                src_ref=source,
                dst_ref=flux_hbm.at[arriving, :],
                send_sem=send_sem.at[k * per + j],
                recv_sem=recv_sem.at[k * per + j],
                device_id={"grp": to},
                device_id_type=MESH,
            )
            copy.start()
            copies.append(copy)
    for copy in heat_copies:
        copy.wait()
    own.wait()
    for copy in copies:
        copy.wait_recv()
    for copy in copies:
        copy.wait_send()


def body(columns, cos_zenith, sunlit, span_map, w_in, w_mid, w_out):
    rows, feat = columns.shape
    groups = lax.axis_size("grp")
    hidden, width = w_out.shape
    levels = width // 2
    tiles = rows // LANES
    anywhere = pl.BlockSpec(memory_space=pl.ANY)
    bf16 = jnp.bfloat16
    heating, flux = pl.pallas_call(
        functools.partial(kernel, groups),
        out_shape=(
            jax.ShapeDtypeStruct((rows, levels), bf16),
            jax.ShapeDtypeStruct((rows, levels), bf16),
        ),
        in_specs=[anywhere] * 7,
        out_specs=(anywhere, anywhere),
        scratch_shapes=[
            pltpu.VMEM((rows, feat), bf16),
            pltpu.VMEM((tiles, LANES), bf16),
            pltpu.VMEM((tiles, LANES), jnp.int32),
            pltpu.VMEM((tiles, LANES), jnp.int32),
            pltpu.VMEM((feat, hidden), bf16),
            pltpu.VMEM((hidden, hidden), bf16),
            pltpu.VMEM((hidden, width), bf16),
            pltpu.VMEM((rows, rows), bf16),
            pltpu.VMEM((rows, LANES), jnp.float32),
            pltpu.VMEM((2, ROWS, hidden), bf16),
            pltpu.VMEM((2, ROWS, hidden), bf16),
            pltpu.VMEM((rows, levels), bf16),
            pltpu.VMEM((rows, levels), bf16),
            pltpu.VMEM((rows, levels), bf16),
            pltpu.SemaphoreType.DMA((7,)),
            pltpu.SemaphoreType.DMA((rows // ROWS,)),
            pltpu.SemaphoreType.DMA,
            pltpu.SemaphoreType.DMA((groups,)),
            pltpu.SemaphoreType.DMA((groups,)),
        ],
        compiler_params=pltpu.CompilerParams(
            collective_id=0, has_side_effects=True, vmem_limit_bytes=40 * 1024 * 1024
        ),
        cost_estimate=pl.CostEstimate(
            flops=2 * rows * (feat * hidden + hidden * hidden + hidden * width),
            bytes_accessed=6 * 1024 * 1024,
            transcendentals=2 * rows * hidden,
        ),
    )(
        columns,
        cos_zenith.reshape(tiles, LANES),
        sunlit.reshape(tiles, LANES),
        span_map.reshape(tiles, LANES),
        w_in,
        w_mid,
        w_out,
    )
    return heating, flux.astype(jnp.float32)


def solution(mesh):
    in_specs = (
        P(("lon", "grp"), None),
        P(("lon", "grp")),
        P(("lon", "grp")),
        P(("lon", "grp")),
        P(),
        P(),
        P(),
    )
    out_specs = (P(("lon", "grp"), None), P(("lon", "grp"), None))
    return jax.shard_map(body, mesh=mesh, in_specs=in_specs, out_specs=out_specs, check_vma=False)
```

time: 76.4 us -> 23.1 us (0.30)
  local copies, waits for them, and re-layouts: 24.7 us -> 7.83 us
  waiting for transfers between devices: 15.4 us -> 0 us
  starting transfers between devices: 13.6 us -> 0 us
  Pallas kernels: 0 us -> 13.4 us
  matrix products: 10.4 us -> 0 us
  blocking collectives: 9.33 us -> 0 us
  other arithmetic: 1.98 us -> 0.83 us
    gather x3 -> x0, local copies, waits for them, and re-layouts: 20.3 us -> none  [the longest x1 8.84 us: body(): sunlit[span_map].reshape(groups, piece_len)]
    all_to_all x3 -> x0, waiting for transfers between devices: 15.4 us -> none  [the longest x1 15.4 us: body(): lax.all_to_all(columns[span_map].reshape(groups, piece_len, columns.shape...]
    all_to_all x3 -> x0, starting transfers between devices: 13.6 us -> none  [the longest x1 5.17 us: body(): lax.all_to_all(cos_zenith[span_map].reshape(groups, piece_len), 'grp', sp...]
    pallas_call x0 -> x1, Pallas kernels: none -> 13.4 us  [body(): pl.pallas_call(functools.partial(kernel, groups), out_shape=(jax.ShapeDty...]
    dot_general x2 -> x0, matrix products: 10.4 us -> none  [the longest x1 6.83 us: network(): jnp.dot(layer_one, w_mid, preferred_element_type=jnp.float32)]
    all_to_all x1 -> x0, blocking collectives: 9.33 us -> none  [body(): lax.all_to_all(phys_heating.reshape(groups, piece_len, levels), 'grp', sp...]
    unnamed x6 -> x15, local copies, waits for them, and re-layouts: 0.02 us -> 7.83 us
    scatter x1 -> x0, local copies, waits for them, and re-layouts: 3.83 us -> none  [body(): heating = jnp.zeros_like(returned).at[span_map].set(returned)]
  transfers between devices with their start and end apart: 3 -> 0, of which waited for: 1 -> 0; matrix products, arithmetic and copies ran while one was open for 18% -> 0% of each run, Pallas kernels for 0% -> 0%
where the time goes in v1:
time: 23.1 us; the launch traced here: 22.7 us
  Pallas kernels  13.4 us (58%)
  local copies, waits for them, and re-layouts  7.83 us (34%)
  other arithmetic  0.83 us (4%)
  between operations  0.66 us (3%)
    pallas_call x1, Pallas kernels, body(): pl.pallas_call(functools.partial(kernel, groups), out_shape=(jax.ShapeDty...  13.4 us
    unnamed x15, local copies, waits for them, and re-layouts  7.83 us
    convert_element_type x1, other arithmetic, body(): return (heating, flux.astype(jnp.float32))  0.83 us

profile of v1, /device:TPU:0, one launch (start us, length us, event | category | flops | bytes accessed | tf_op | source)
XLA Modules:
  0.0 22.7 jit_solution(6905529346650421378)
XLA Ops:
  0.6 0.0 copy-start
  0.6 1.6 %copy-done = bf16[1024,1024]{1,0:T(8,128)(2,1)S(1)} copy-done((bf16[1024,1024]{1,0:T(8,128)(2,1)S(1)}, bf16[1024,1024]{1,0:T(8,128)(2,1)}, u32[]{:S(2)}) %copy-start) | copy-done | bytes 2097176
  2.2 0.0 copy-start.1
  2.2 1.2 %copy-done.1 = bf16[1024,512]{1,0:T(8,128)(2,1)S(1)} copy-done((bf16[1024,512]{1,0:T(8,128)(2,1)S(1)}, bf16[1024,512]{1,0:T(8,128)(2,1)}, u32[]{:S(2)}) %copy-start.1) | copy-done | bytes 1048600
  3.4 0.0 copy-start.2
  3.5 1.2 %copy-done.2 = bf16[512,1024]{1,0:T(8,128)(2,1)S(1)} copy-done((bf16[512,1024]{1,0:T(8,128)(2,1)S(1)}, bf16[512,1024]{1,0:T(8,128)(2,1)}, u32[]{:S(2)}) %copy-start.2) | copy-done | bytes 1048600
  4.7 0.0 copy-start.3
  4.7 1.0 %copy-done.3 = bf16[1024,256]{1,0:T(8,128)(2,1)S(1)} copy-done((bf16[1024,256]{1,0:T(8,128)(2,1)S(1)}, bf16[1024,256]{1,0:T(8,128)(2,1)}, u32[]{:S(2)}) %copy-start.3) | copy-done | bytes 524312
  5.7 0.0 copy-start.4
  5.7 0.7 %copy-done.4 = s32[1024]{0:T(1024)S(1)} copy-done((s32[1024]{0:T(1024)S(1)}, s32[1024]{0:T(1024)}, u32[]{:S(2)}) %copy-start.4) | copy-done | bytes 4120
  6.4 0.0 copy-start.5
  6.4 0.7 %copy-done.5 = s32[1024]{0:T(1024)S(1)} copy-done((s32[1024]{0:T(1024)S(1)}, s32[1024]{0:T(1024)}, u32[]{:S(2)}) %copy-start.5) | copy-done | bytes 4120
  7.1 0.0 copy-start.6
  7.1 0.7 %copy-done.6 = bf16[1024]{0:T(1024)(128)(2,1)S(1)} copy-done((bf16[1024]{0:T(1024)(128)(2,1)S(1)}, bf16[1024]{0:T(1024)(128)(2,1)}, u32[]{:S(2)}) %copy-start.6) | copy-done | bytes 2072
  7.8 13.4 %shard_map.86 = (bf16[1024,128]{1,0:T(8,128)(2,1)S(1)}, bf16[1024,128]{1,0:T(8,128)(2,1)S(1)}) custom-call(bf16[1024,512]{1,0:T(8,128)(2,1)S(1)} %copy-done.1, bf16[8,128]{1,0:T(8,128)(2,1)S(1)} %bitcast.5, s32[8,128]{1,0:T(8,128)S(1)} %bitcast.3, s32[8,128]{1,0:T(8,128)S(1)} %bitcast.4, bf16[512,1024]{1,0:T(8,128)(2,1)S(1)} %copy-done.2, ...), custom_call_target="tpu_custom_call" | custom-call | flops 3758096384 | bytes 6291456 | tf_op jit(solution)/shard_map/pallas_call | solution.py:145
  21.2 0.8 %convert_element_type.3 = f32[1024,128]{1,0:T(8,128)} convert(bf16[1024,128]{1,0:T(8,128)(2,1)S(1)} %get-tuple-element.5) | non-fusion elementwise | flops 131072 | bytes 786432 | tf_op jit(solution)/shard_map/convert_element_type | solution.py:191
  22.0 0.7 %copy.10 = bf16[1024,128]{1,0:T(8,128)(2,1)} copy(bf16[1024,128]{1,0:T(8,128)(2,1)S(1)} %get-tuple-element.8) | data formatting | bytes 524288
Async XLA Ops:
  0.6 1.6 %copy-start = (bf16[1024,1024]{1,0:T(8,128)(2,1)S(1)}, bf16[1024,1024]{1,0:T(8,128)(2,1)}, u32[]{:S(2)}) copy-start(bf16[1024,1024]{1,0:T(8,128)(2,1)} %w_mid_hbm.1) | copy-start | bytes 6291460
  2.2 1.2 %copy-start.1 = (bf16[1024,512]{1,0:T(8,128)(2,1)S(1)}, bf16[1024,512]{1,0:T(8,128)(2,1)}, u32[]{:S(2)}) copy-start(bf16[1024,512]{1,0:T(8,128)(2,1)} %columns_hbm.1) | copy-start | bytes 3145732
  3.4 1.2 %copy-start.2 = (bf16[512,1024]{1,0:T(8,128)(2,1)S(1)}, bf16[512,1024]{1,0:T(8,128)(2,1)}, u32[]{:S(2)}) copy-start(bf16[512,1024]{1,0:T(8,128)(2,1)} %w_in_hbm.1) | copy-start | bytes 3145732
  4.7 1.0 %copy-start.3 = (bf16[1024,256]{1,0:T(8,128)(2,1)S(1)}, bf16[1024,256]{1,0:T(8,128)(2,1)}, u32[]{:S(2)}) copy-start(bf16[1024,256]{1,0:T(8,128)(2,1)} %w_out_hbm.1) | copy-start | bytes 1572868
  5.7 0.7 %copy-start.4 = (s32[1024]{0:T(1024)S(1)}, s32[1024]{0:T(1024)}, u32[]{:S(2)}) copy-start(s32[1024]{0:T(1024)} %param.9) | copy-start | bytes 12292
  6.4 0.7 %copy-start.5 = (s32[1024]{0:T(1024)S(1)}, s32[1024]{0:T(1024)}, u32[]{:S(2)}) copy-start(s32[1024]{0:T(1024)} %param.10) | copy-start | bytes 12292
  7.1 0.7 %copy-start.6 = (bf16[1024]{0:T(1024)(128)(2,1)S(1)}, bf16[1024]{0:T(1024)(128)(2,1)}, u32[]{:S(2)}) copy-start(bf16[1024]{0:T(1024)(128)(2,1)} %param.8) | copy-start | bytes 6148

commit v2 on v1

--- a/solution.py
+++ b/solution.py
@@ -30,10 +30,10 @@
 def kernel(
     groups,
     columns_hbm, cos_hbm, sun_hbm, map_hbm, w_in_hbm, w_mid_hbm, w_out_hbm,
-    heat_hbm, flux_hbm,
+    heat_ref, flux_ref,
     columns, cos, sun, smap, w_in, w_mid, w_out,
-    onehot, insol, layer_one, layer_two, heat, flux, leaving,
-    load_sem, heat_sem, own_sem, send_sem, recv_sem,
+    onehot, back, insol, gathered, layer_one, layer_two, heat, leaving,
+    load_sem, own_sem, send_sem, recv_sem,
 ):
     rows = columns.shape[0]
     hidden = w_in.shape[1]
@@ -67,57 +67,52 @@
     lane = lax.broadcasted_iota(jnp.int32, (LANES, LANES), 1).astype(jnp.float32)
     for at in range(rows // LANES):
         here = pl.ds(at * LANES, LANES)
-        insol[here, :] = down(light[at : at + 1, :])
         wanted = down(slots[at : at + 1, :])
+        lit = jnp.zeros((LANES, LANES), jnp.float32)
         for k in range(rows // LANES):
-            onehot[here, k * LANES : (k + 1) * LANES] = jnp.where(
-                wanted == lane + float(k * LANES), 1.0, 0.0
-            ).astype(jnp.bfloat16)
+            hit = wanted == lane + float(k * LANES)
+            onehot[here, k * LANES : (k + 1) * LANES] = jnp.where(hit, 1.0, 0.0).astype(jnp.bfloat16)
+            lit = lit + jnp.where(hit, light[k : k + 1, :], 0.0)
+        insol[here, :] = jnp.broadcast_to(jnp.sum(lit, axis=1, keepdims=True), (LANES, LANES))
 
     loads[3].wait()
     loads[4].wait()
-    heat_copies = []
-    for at in range(rows // ROWS):
-        here = pl.ds(at * ROWS, ROWS)
-        for n in range(0, hidden, WIDE):
-            layer_one[at % 2, :, n : n + WIDE] = silu(
-                jnp.dot(columns[here, :], w_in[:, n : n + WIDE], preferred_element_type=jnp.float32)
-            ).astype(jnp.bfloat16)
-        if at == 0:
-            loads[5].wait()
-        for n in range(0, hidden, WIDE):
-            layer_two[at % 2, :, n : n + WIDE] = silu(
-                jnp.dot(layer_one[at % 2], w_mid[:, n : n + WIDE], preferred_element_type=jnp.float32)
-            ).astype(jnp.bfloat16)
-        if at == 0:
-            loads[6].wait()
-        out = jnp.dot(layer_two[at % 2], w_out[...], preferred_element_type=jnp.float32)
-        heat[here, :] = (insol[here, :] * out[:, :levels]).astype(jnp.bfloat16)
-        flux[here, :] = (insol[here, :] * softplus(out[:, levels:])).astype(jnp.bfloat16)
-        copy = pltpu.make_async_copy(heat.at[here, :], heat_hbm.at[here, :], heat_sem.at[at])
-        copy.start()
-        heat_copies.append(copy)
-
-    pl.semaphore_wait(barrier, groups - 1)
     copies = []
     own = None
     arriving = pl.ds(pl.multiple_of(me * piece, piece), piece)
     for k in range(PARTS):
         part = lax.rem(my_part + k + 1, PARTS)
         here = pl.ds(pl.multiple_of(part * part_rows, part_rows), part_rows)
-        leaving[here, :] = jnp.dot(
-            onehot[here, :], flux[...], preferred_element_type=jnp.float32
+        gathered[k % 2] = jnp.dot(
+            onehot[here, :], columns[...], preferred_element_type=jnp.float32
         ).astype(jnp.bfloat16)
+        for n in range(0, hidden, WIDE):
+            layer_one[k % 2, :, n : n + WIDE] = silu(
+                jnp.dot(gathered[k % 2], w_in[:, n : n + WIDE], preferred_element_type=jnp.float32)
+            ).astype(jnp.bfloat16)
+        if k == 0:
+            loads[5].wait()
+        for n in range(0, hidden, WIDE):
+            layer_two[k % 2, :, n : n + WIDE] = silu(
+                jnp.dot(layer_one[k % 2], w_mid[:, n : n + WIDE], preferred_element_type=jnp.float32)
+            ).astype(jnp.bfloat16)
+        if k == 0:
+            loads[6].wait()
+        out = jnp.dot(layer_two[k % 2], w_out[...], preferred_element_type=jnp.float32)
+        leaving[here, :] = (insol[here, :] * softplus(out[:, levels:])).astype(jnp.bfloat16)
+        heat[here, :] = (insol[here, :] * out[:, :levels]).astype(jnp.bfloat16)
+        if k == 0:
+            pl.semaphore_wait(barrier, groups - 1)
         for j in range(per):
             to = part * per + lax.rem(my_place + j, per)
             source = leaving.at[pl.ds(pl.multiple_of(to * piece, piece), piece), :]
             if k == PARTS - 1 and j == 0:
-                own = pltpu.make_async_copy(source, flux_hbm.at[arriving, :], own_sem)
+                own = pltpu.make_async_copy(source, flux_ref.at[arriving, :], own_sem)
                 own.start()
                 continue
             copy = pltpu.make_async_remote_copy(
                 src_ref=source,
-                dst_ref=flux_hbm.at[arriving, :],
+                dst_ref=flux_ref.at[arriving, :],
                 send_sem=send_sem.at[k * per + j],
                 recv_sem=recv_sem.at[k * per + j],
                 device_id={"grp": to},
@@ -125,8 +120,18 @@
             )
             copy.start()
             copies.append(copy)
-    for copy in heat_copies:
-        copy.wait()
+        if k == 0:
+            column = lax.broadcasted_iota(jnp.int32, (LANES, LANES), 0).astype(jnp.float32)
+            for at in range(rows // LANES):
+                for s in range(rows // LANES):
+                    back[at * LANES : (at + 1) * LANES, s * LANES : (s + 1) * LANES] = jnp.where(
+                        slots[s : s + 1, :] == column + float(at * LANES), 1.0, 0.0
+                    ).astype(jnp.bfloat16)
+    for at in range(rows // ROWS):
+        here = pl.ds(at * ROWS, ROWS)
+        heat_ref[here, :] = jnp.dot(
+            back[here, :], heat[...], preferred_element_type=jnp.float32
+        ).astype(jnp.bfloat16)
     own.wait()
     for copy in copies:
         copy.wait_recv()
@@ -145,11 +150,11 @@
     heating, flux = pl.pallas_call(
         functools.partial(kernel, groups),
         out_shape=(
-            jax.ShapeDtypeStruct((rows, levels), bf16),
-            jax.ShapeDtypeStruct((rows, levels), bf16),
+            pltpu.VMEM((rows, levels), bf16),
+            pltpu.VMEM((rows, levels), bf16),
         ),
         in_specs=[anywhere] * 7,
-        out_specs=(anywhere, anywhere),
+        out_specs=(pl.BlockSpec(memory_space=pltpu.VMEM),) * 2,
         scratch_shapes=[
             pltpu.VMEM((rows, feat), bf16),
             pltpu.VMEM((tiles, LANES), bf16),
@@ -159,20 +164,20 @@
             pltpu.VMEM((hidden, hidden), bf16),
             pltpu.VMEM((hidden, width), bf16),
             pltpu.VMEM((rows, rows), bf16),
+            pltpu.VMEM((rows, rows), bf16),
             pltpu.VMEM((rows, LANES), jnp.float32),
-            pltpu.VMEM((2, ROWS, hidden), bf16),
-            pltpu.VMEM((2, ROWS, hidden), bf16),
-            pltpu.VMEM((rows, levels), bf16),
+            pltpu.VMEM((2, rows // PARTS, feat), bf16),
+            pltpu.VMEM((2, rows // PARTS, hidden), bf16),
+            pltpu.VMEM((2, rows // PARTS, hidden), bf16),
             pltpu.VMEM((rows, levels), bf16),
             pltpu.VMEM((rows, levels), bf16),
             pltpu.SemaphoreType.DMA((7,)),
-            pltpu.SemaphoreType.DMA((rows // ROWS,)),
             pltpu.SemaphoreType.DMA,
             pltpu.SemaphoreType.DMA((groups,)),
             pltpu.SemaphoreType.DMA((groups,)),
         ],
         compiler_params=pltpu.CompilerParams(
-            collective_id=0, has_side_effects=True, vmem_limit_bytes=40 * 1024 * 1024
+            collective_id=0, has_side_effects=True, vmem_limit_bytes=62 * 1024 * 1024
         ),
         cost_estimate=pl.CostEstimate(
             flops=2 * rows * (feat * hidden + hidden * hidden + hidden * width),

time: 23.1 us -> 15.1 us (0.65)
  local copies, waits for them, and re-layouts: 7.83 us -> 0.71 us
  Pallas kernels: 13.4 us -> 12.8 us
    unnamed x15 -> x1, local copies, waits for them, and re-layouts: 7.83 us -> 0.71 us
    pallas_call x1, Pallas kernels: 13.4 us -> 12.8 us  [body(): pl.pallas_call(functools.partial(kernel, groups), out_shape=(pltpu.VMEM((...]
where the time goes in v2:
time: 15.1 us; the launch traced here: 14.9 us
  Pallas kernels  12.8 us (85%)
  other arithmetic  0.83 us (5%)
  local copies, waits for them, and re-layouts  0.71 us (5%)
  between operations  0.64 us (4%)
    pallas_call x1, Pallas kernels, body(): pl.pallas_call(functools.partial(kernel, groups), out_shape=(pltpu.VMEM((...  12.8 us
    convert_element_type x1, other arithmetic, body(): return (heating, flux.astype(jnp.float32))  0.83 us
    unnamed x1, local copies, waits for them, and re-layouts  0.71 us

profile of v2, /device:TPU:0, one launch (start us, length us, event | category | flops | bytes accessed | tf_op | source)
XLA Modules:
  0.0 14.9 jit_solution(14622221599116457714)
XLA Ops:
  0.6 12.8 %shard_map.86 = (bf16[1024,128]{1,0:T(8,128)(2,1)S(1)}, bf16[1024,128]{1,0:T(8,128)(2,1)S(1)}) custom-call(bf16[1024,512]{1,0:T(8,128)(2,1)} %columns_hbm.1, bf16[8,128]{1,0:T(8,128)(2,1)} %bitcast.5, s32[8,128]{1,0:T(8,128)} %bitcast.3, s32[8,128]{1,0:T(8,128)} %bitcast.4, bf16[512,1024]{1,0:T(8,128)(2,1)} %w_in_hbm.1, bf16[1024,1024]{1,0:T(8,128)(2,1)} %w_mid_hbm.1, ...), custom_call_target="tpu_custom_call" | custom-call | flops 3758096384 | bytes 6291456 | tf_op jit(solution)/shard_map/pallas_call | solution.py:150
  13.4 0.7 %copy.10 = bf16[1024,128]{1,0:T(8,128)(2,1)} copy(bf16[1024,128]{1,0:T(8,128)(2,1)S(1)} %get-tuple-element.6) | data formatting | bytes 524288
  14.1 0.8 %convert_element_type.3 = f32[1024,128]{1,0:T(8,128)} convert(bf16[1024,128]{1,0:T(8,128)(2,1)S(1)} %get-tuple-element.5) | non-fusion elementwise | flops 131072 | bytes 786432 | tf_op jit(solution)/shard_map/convert_element_type | solution.py:196

commit v3 on v2

--- a/solution.py
+++ b/solution.py
@@ -12,6 +12,7 @@
 ROWS = 256
 WIDE = 256
 PARTS = 4
+FINISH = 4
 
 
 def silu(v):
@@ -52,7 +53,7 @@
 
     pairs = (
         (map_hbm, smap), (cos_hbm, cos), (sun_hbm, sun),
-        (w_in_hbm, w_in), (columns_hbm, columns), (w_mid_hbm, w_mid), (w_out_hbm, w_out),
+        (columns_hbm, columns), (w_in_hbm, w_in), (w_mid_hbm, w_mid), (w_out_hbm, w_out),
     )
     loads = [
         pltpu.make_async_copy(src, dst, load_sem.at[at]) for at, (src, dst) in enumerate(pairs)
@@ -62,40 +63,71 @@
 
     for load in loads[:3]:
         load.wait()
+    blocks = rows // LANES
+    inside = part_rows // LANES
     slots = smap[...].astype(jnp.float32)
     light = sun[...].astype(jnp.float32) * cos[...].astype(jnp.float32)
     lane = lax.broadcasted_iota(jnp.int32, (LANES, LANES), 1).astype(jnp.float32)
-    for at in range(rows // LANES):
-        here = pl.ds(at * LANES, LANES)
-        wanted = down(slots[at : at + 1, :])
+    column = lax.broadcasted_iota(jnp.int32, (LANES, LANES), 0).astype(jnp.float32)
+
+    def part_of(k):
+        return lax.rem(my_part + k + 1, PARTS)
+
+    def pick(k, at):
+        block = part_of(k) * inside + at
+        wanted = down(smap[pl.ds(block, 1), :].astype(jnp.float32))
+        here = pl.ds(pl.multiple_of(block * LANES, LANES), LANES)
         lit = jnp.zeros((LANES, LANES), jnp.float32)
-        for k in range(rows // LANES):
-            hit = wanted == lane + float(k * LANES)
-            onehot[here, k * LANES : (k + 1) * LANES] = jnp.where(hit, 1.0, 0.0).astype(jnp.bfloat16)
-            lit = lit + jnp.where(hit, light[k : k + 1, :], 0.0)
+        for b in range(blocks):
+            hit = wanted == lane + float(b * LANES)
+            onehot[here, b * LANES : (b + 1) * LANES] = jnp.where(hit, 1.0, 0.0).astype(jnp.bfloat16)
+            lit = lit + jnp.where(hit, light[b : b + 1, :], 0.0)
         insol[here, :] = jnp.broadcast_to(jnp.sum(lit, axis=1, keepdims=True), (LANES, LANES))
 
+    def put(at, s):
+        back[at * LANES : (at + 1) * LANES, s * LANES : (s + 1) * LANES] = jnp.where(
+            slots[s : s + 1, :] == column + float(at * LANES), 1.0, 0.0
+        ).astype(jnp.bfloat16)
+
+    for at in range(inside):
+        pick(0, at)
     loads[3].wait()
-    loads[4].wait()
     copies = []
     own = None
     arriving = pl.ds(pl.multiple_of(me * piece, piece), piece)
     for k in range(PARTS):
-        part = lax.rem(my_part + k + 1, PARTS)
+        part = part_of(k)
         here = pl.ds(pl.multiple_of(part * part_rows, part_rows), part_rows)
         gathered[k % 2] = jnp.dot(
             onehot[here, :], columns[...], preferred_element_type=jnp.float32
         ).astype(jnp.bfloat16)
+        jobs = [
+            functools.partial(put, at, s)
+            for at in range(k * inside, (k + 1) * inside)
+            for s in range(blocks)
+        ]
+        if k + 1 < PARTS:
+            jobs += [functools.partial(pick, k + 1, at) for at in range(inside)]
+        tiles = hidden // WIDE
+        share = -(-len(jobs) // (2 * tiles))
+        if k == 0:
+            loads[4].wait()
         for n in range(0, hidden, WIDE):
             layer_one[k % 2, :, n : n + WIDE] = silu(
                 jnp.dot(gathered[k % 2], w_in[:, n : n + WIDE], preferred_element_type=jnp.float32)
             ).astype(jnp.bfloat16)
+            for job in jobs[:share]:
+                job()
+            jobs = jobs[share:]
         if k == 0:
             loads[5].wait()
         for n in range(0, hidden, WIDE):
             layer_two[k % 2, :, n : n + WIDE] = silu(
                 jnp.dot(layer_one[k % 2], w_mid[:, n : n + WIDE], preferred_element_type=jnp.float32)
             ).astype(jnp.bfloat16)
+            for job in jobs[:share]:
+                job()
+            jobs = jobs[share:]
         if k == 0:
             loads[6].wait()
         out = jnp.dot(layer_two[k % 2], w_out[...], preferred_element_type=jnp.float32)
@@ -120,13 +152,6 @@
             )
             copy.start()
             copies.append(copy)
-        if k == 0:
-            column = lax.broadcasted_iota(jnp.int32, (LANES, LANES), 0).astype(jnp.float32)
-            for at in range(rows // LANES):
-                for s in range(rows // LANES):
-                    back[at * LANES : (at + 1) * LANES, s * LANES : (s + 1) * LANES] = jnp.where(
-                        slots[s : s + 1, :] == column + float(at * LANES), 1.0, 0.0
-                    ).astype(jnp.bfloat16)
     for at in range(rows // ROWS):
         here = pl.ds(at * ROWS, ROWS)
         heat_ref[here, :] = jnp.dot(
@@ -137,6 +162,20 @@
         copy.wait_recv()
     for copy in copies:
         copy.wait_send()
+
+
+def finish(heat, flux, heat_hbm, flux_hbm, wide, sem):
+    copies = [pltpu.make_async_copy(heat, heat_hbm, sem.at[FINISH])]
+    copies[0].start()
+    step = flux.shape[0] // FINISH
+    for at in range(FINISH):
+        here = pl.ds(at * step, step)
+        wide[here, :] = flux[here, :].astype(jnp.float32)
+        copy = pltpu.make_async_copy(wide.at[here, :], flux_hbm.at[here, :], sem.at[at])
+        copy.start()
+        copies.append(copy)
+    for copy in copies:
+        copy.wait()
 
 
 def body(columns, cos_zenith, sunlit, span_map, w_in, w_mid, w_out):
@@ -193,7 +232,20 @@
         w_mid,
         w_out,
     )
-    return heating, flux.astype(jnp.float32)
+    return pl.pallas_call(
+        finish,
+        out_shape=(
+            jax.ShapeDtypeStruct((rows, levels), bf16),
+            jax.ShapeDtypeStruct((rows, levels), jnp.float32),
+        ),
+        in_specs=[pl.BlockSpec(memory_space=pltpu.VMEM)] * 2,
+        out_specs=(anywhere, anywhere),
+        scratch_shapes=[
+            pltpu.VMEM((rows, levels), jnp.float32),
+            pltpu.SemaphoreType.DMA((FINISH + 1,)),
+        ],
+        compiler_params=pltpu.CompilerParams(vmem_limit_bytes=4 * 1024 * 1024),
+    )(heating, flux)
 
 
 def solution(mesh):

time: 15.1 us -> 14.3 us (0.947)
  other arithmetic: 0.83 us -> 0 us
  local copies, waits for them, and re-layouts: 0.71 us -> 0 us
  Pallas kernels: 12.8 us -> 13.5 us
    pallas_call x0 -> x1, Pallas kernels: none -> 0.92 us  [body(): pl.pallas_call(finish, out_shape=(jax.ShapeDtypeStruct((rows, levels), bf...]
    convert_element_type x1 -> x0, other arithmetic: 0.83 us -> none  [body(): return (heating, flux.astype(jnp.float32))]
    unnamed x1 -> x0, local copies, waits for them, and re-layouts: 0.71 us -> none
    pallas_call x1, Pallas kernels: 12.8 us -> 12.6 us  [body(): pl.pallas_call(functools.partial(kernel, groups), out_shape=(pltpu.VMEM((...]
where the time goes in v3:
time: 14.3 us; the launch traced here: 14.2 us
  Pallas kernels  13.5 us (94%)
  between operations  0.64 us (4%)
    pallas_call x1, Pallas kernels, body(): pl.pallas_call(functools.partial(kernel, groups), out_shape=(pltpu.VMEM((...  12.6 us
    pallas_call x1, Pallas kernels, body(): pl.pallas_call(finish, out_shape=(jax.ShapeDtypeStruct((rows, levels), bf...  0.92 us

profile of v3, /device:TPU:0, one launch (start us, length us, event | category | flops | bytes accessed | tf_op | source)
XLA Modules:
  0.0 14.2 jit_solution(315906829281564069)
XLA Ops:
  0.6 12.6 %shard_map.86 = (bf16[1024,128]{1,0:T(8,128)(2,1)S(1)}, bf16[1024,128]{1,0:T(8,128)(2,1)S(1)}) custom-call(bf16[1024,512]{1,0:T(8,128)(2,1)} %columns_hbm.1, bf16[8,128]{1,0:T(8,128)(2,1)} %bitcast.5, s32[8,128]{1,0:T(8,128)} %bitcast.3, s32[8,128]{1,0:T(8,128)} %bitcast.4, bf16[512,1024]{1,0:T(8,128)(2,1)} %w_in_hbm.1, bf16[1024,1024]{1,0:T(8,128)(2,1)} %w_mid_hbm.1, ...), custom_call_target="tpu_custom_call" | custom-call | flops 3758096384 | bytes 6291456 | tf_op jit(solution)/shard_map/pallas_call | solution.py:189
  13.2 0.9 %shard_map.87 = (bf16[1024,128]{1,0:T(8,128)(2,1)}, f32[1024,128]{1,0:T(8,128)}) custom-call(bf16[1024,128]{1,0:T(8,128)(2,1)S(1)} %get-tuple-element.4.heat, bf16[1024,128]{1,0:T(8,128)(2,1)S(1)} %get-tuple-element.5.flux), custom_call_target="tpu_custom_call" | custom-call | tf_op jit(solution)/shard_map/pallas_call | solution.py:235

commit v4 on v3

--- a/solution.py
+++ b/solution.py
@@ -98,9 +98,10 @@
     for k in range(PARTS):
         part = part_of(k)
         here = pl.ds(pl.multiple_of(part * part_rows, part_rows), part_rows)
-        gathered[k % 2] = jnp.dot(
-            onehot[here, :], columns[...], preferred_element_type=jnp.float32
-        ).astype(jnp.bfloat16)
+        for n in range(0, columns.shape[1], WIDE):
+            gathered[k % 2, :, n : n + WIDE] = jnp.dot(
+                onehot[here, :], columns[:, n : n + WIDE], preferred_element_type=jnp.float32
+            ).astype(jnp.bfloat16)
         jobs = [
             functools.partial(put, at, s)
             for at in range(k * inside, (k + 1) * inside)

time: 14.3 us -> 14.3 us (level)
  no operation moved by 1% of the time
where the time goes in v4:
time: 14.3 us; the launch traced here: 14.2 us
  Pallas kernels  13.5 us (94%)
  between operations  0.64 us (4%)
    pallas_call x1, Pallas kernels, body(): pl.pallas_call(functools.partial(kernel, groups), out_shape=(pltpu.VMEM((...  12.6 us
    pallas_call x1, Pallas kernels, body(): pl.pallas_call(finish, out_shape=(jax.ShapeDtypeStruct((rows, levels), bf...  0.92 us

profile of v4, /device:TPU:0, one launch (start us, length us, event | category | flops | bytes accessed | tf_op | source)
XLA Modules:
  0.0 14.2 jit_solution(315906829281564069)
XLA Ops:
  0.6 12.6 %shard_map.86 = (bf16[1024,128]{1,0:T(8,128)(2,1)S(1)}, bf16[1024,128]{1,0:T(8,128)(2,1)S(1)}) custom-call(bf16[1024,512]{1,0:T(8,128)(2,1)} %columns_hbm.1, bf16[8,128]{1,0:T(8,128)(2,1)} %bitcast.5, s32[8,128]{1,0:T(8,128)} %bitcast.3, s32[8,128]{1,0:T(8,128)} %bitcast.4, bf16[512,1024]{1,0:T(8,128)(2,1)} %w_in_hbm.1, bf16[1024,1024]{1,0:T(8,128)(2,1)} %w_mid_hbm.1, ...), custom_call_target="tpu_custom_call" | custom-call | flops 3758096384 | bytes 6291456 | tf_op jit(solution)/shard_map/pallas_call | solution.py:190
  13.2 0.9 %shard_map.87 = (bf16[1024,128]{1,0:T(8,128)(2,1)}, f32[1024,128]{1,0:T(8,128)}) custom-call(bf16[1024,128]{1,0:T(8,128)(2,1)S(1)} %get-tuple-element.4.heat, bf16[1024,128]{1,0:T(8,128)(2,1)S(1)} %get-tuple-element.5.flux), custom_call_target="tpu_custom_call" | custom-call | tf_op jit(solution)/shard_map/pallas_call | solution.py:236
